TPU v7x, 128 devices: a whole 4x4x4 slice. The times are simulated.
128 devices in a mesh: row: 4 (over y_hi, core), col: 32 (over x, z, y_lo).
Axes of the slice: x: 4, y: 4 (y_hi: 2, y_lo: 2; y = y_hi * 2 + y_lo), z: 4, core: 2. Of those that a mesh axis runs over, the one named last changes fastest.
Arguments:
- pair: bfloat16 [768, 768, 128], P('row', 'col'), may hold values from -6 to 6
- norm_in: float32 [2, 128], replicated, may hold values from 0.1 to 1.9
- proj_weight: bfloat16 [2, 128, 512], replicated, may hold values from -0.5 to 0.5
- gate_weight: bfloat16 [2, 128, 128], replicated, may hold values from -0.5 to 0.5
- norm_out: float32 [2, 128], replicated, may hold values from 0.1 to 1.9
- out_weight: bfloat16 [2, 128, 128], replicated, may hold values from -0.5 to 0.5
Outputs:
- updated_pair: bfloat16 [768, 768, 128], P('row', 'col')
All inputs are finite; a program needn't handle non-finite values.
Results may differ from a plain program's by a relative error of at most 0.018.
Values may be sent and summed in bfloat16 or wider, within the bound.
A program may use at most 64 MiB of HBM per device.

v0:
```python
import functools

import jax
import jax.numpy as jnp
from jax import lax
from jax.experimental import pallas as pl
from jax.experimental.pallas import tpu as pltpu
from jax.sharding import PartitionSpec as P

F32, BF16 = jnp.float32, jnp.bfloat16
MESH = pl.DeviceIdType.MESH

ROWS, COLS, C = 192, 24, 128
CHIPS = 64
PAIRS = 18
TOKENS = 768


def chip_coords():
    row, col = lax.axis_index("row"), lax.axis_index("col")
    return col // 8, (row // 2) * 2 + col % 2, (col // 2) % 4, row % 2


def peer(step, x, y, z):
    s = lax.rem(step * 37, CHIPS)
    px = lax.rem(x + s // 16, 4)
    py = lax.rem(y + lax.rem(s // 4, 4), 4)
    pz = lax.rem(z + lax.rem(s, 4), 4)
    return py // 2, px * 8 + pz * 2 + lax.rem(py, 2)


def norm_cols(values, gain):
    mean = jnp.mean(values, 0, keepdims=True)
    centered = values - mean
    variance = jnp.mean(centered * centered, 0, keepdims=True)
    return centered * lax.rsqrt(variance + 1e-05) * gain


def kernel(
    pair, norm_in, proj_w, gate_w, norm_out, out_w, out,
    zt, nb, gate, msg, left_right0, left_right1, xs, xr, part_out, part_in, part_own, ret, mix0, mix1, work,
    wfa, wfb, proj_a, gate_a, out_a, gain_in, gain_out, x2,
    fwd_send, fwd_recv, ret_send, ret_recv, core_send, core_recv,
):
    x, y, z, core = chip_coords()
    y_hi = y // 2
    col = lax.axis_index("col")
    me = y_hi * 32 + col
    sibling = (y_hi * 2 + 1 - core, col)

    def pick(a, b):
        return jnp.where(lax.broadcasted_iota(jnp.int32, a.shape, 1) < 64, a, b)

    barrier = pltpu.get_barrier_semaphore()
    pl.semaphore_signal(barrier, inc=1, device_id=sibling, device_id_type=MESH)

    @pl.loop(1, CHIPS)
    def _(step):
        py, pc = peer(step, x, y, z)
        pl.semaphore_signal(barrier, inc=1, device_id=(py * 2 + core, pc), device_id_type=MESH)

    for p in range(2):
        wt = proj_w[p].astype(F32).T
        wfa[...] = jnp.zeros_like(wfa)
        wfb[...] = jnp.zeros_like(wfb)
        wfa[pl.ds(0, 512, stride=2), :] = wt
        wfb[pl.ds(1, 512, stride=2), :] = wt
        proj_a[p, :, 0:128] = wfa[...].astype(BF16)
        proj_a[p, :, 128:256] = wfb[...].astype(BF16)
        gt = gate_w[p].astype(F32).T.astype(BF16)
        wfa[pl.ds(0, 64, stride=2), :] = out_w[p, 0:64].astype(F32)
        wfa[pl.ds(1, 64, stride=2), :] = out_w[p, 64:128].astype(F32)
        ot = wfa[0:128].T.astype(BF16)
        zero = jnp.zeros((128, 128), BF16)
        for dst, block in ((gate_a, gt), (out_a, ot)):
            dst[p, 0:128, 0:128] = block
            dst[p, 0:128, 128:256] = zero
            dst[p, 128:256, 0:128] = zero
            dst[p, 128:256, 128:256] = block
        picked = lax.broadcasted_iota(jnp.int32, (2, 128), 0) == p
        gain = jnp.sum(jnp.where(picked, norm_in[...], 0.0), 0, keepdims=True)
        gain_in[p] = jnp.broadcast_to(gain, (128, 128)).T
        gain = jnp.sum(jnp.where(picked, norm_out[...], 0.0), 0, keepdims=True)
        gain = jnp.broadcast_to(gain, (128, 128)).T
        wfa[pl.ds(0, 64, stride=2), :] = gain[0:64]
        wfa[pl.ds(1, 64, stride=2), :] = gain[64:128]
        gain_out[p] = wfa[0:128]

    work[...] = pair[...].astype(F32)

    @pl.loop(0, 12)
    def _(tp):
        for e in range(2):
            zt[tp, e * 128:(e + 1) * 128] = work[pl.ds(2 * tp + e, 128, stride=24), :].T.astype(BF16)

    @pl.loop(0, 6)
    def _(tp):
        for e in range(2):
            m = 2 * tp + e
            a = work[pl.ds(128 * 24 + m + 12 * y_hi, 64, stride=24), :]
            b = work[pl.ds(128 * 24 + m + 12 * (1 - y_hi), 64, stride=24), :]
            zt[12 + tp, e * 128:(e + 1) * 128] = jnp.concatenate([a, b], 0).T.astype(BF16)

    def project(p, u):
        for e in range(2):
            tp = 2 * u + e
            for h in range(2):
                rows = slice(h * 128, (h + 1) * 128)
                nb[tp, rows] = norm_cols(zt[tp, rows].astype(F32), gain_in[p]).astype(BF16)
        n = jnp.concatenate([nb[2 * u], nb[2 * u + 1]], 1)
        for side in range(2):
            a = proj_a[p, side * 512:(side + 1) * 512]
            got = jnp.dot(a, n, preferred_element_type=F32)
            val = (jax.nn.sigmoid(got[256:512]) * got[0:256]).astype(BF16)
            for ab in range(2):
                for e in range(2):
                    block = val[ab * 128:(ab + 1) * 128, e * 128:(e + 1) * 128]
                    msg[ab * 2 + side, 2 * u + e] = block.reshape(64, 2, 128)

    def gates(p):
        @pl.loop(0, 9)
        def _(u):
            n = jnp.concatenate([nb[2 * u], nb[2 * u + 1]], 1)
            g = jax.nn.sigmoid(jnp.dot(gate_a[p], n, preferred_element_type=F32))
            gate[2 * u] = g[:, 0:128]
            gate[2 * u + 1] = g[:, 128:256]

    def send_all(src_of, dst, send, recv):
        @pl.loop(1, CHIPS)
        def _(step):
            py, pc = peer(step, x, y, z)
            pltpu.make_async_remote_copy(
                src_ref=src_of(py * 32 + pc), dst_ref=dst, send_sem=send, recv_sem=recv,
                device_id=(py * 2 + core, pc), device_id_type=MESH,
            ).start()
        pltpu.make_async_copy(src_of(me), dst, recv).start()

    def wait_bytes(ref, sem):
        pltpu.make_async_copy(ref, ref, sem).wait()

    def build(src, i):
        t = src[i, 0:32, 12:18].reshape(384, 128).astype(F32)
        v = src[i, 32:64, 12:18].reshape(384, 128).astype(F32)
        xs[i, :, 0:128] = src[i, 0:32, 0:12].reshape(768, 128)
        xs[i, :, 128:256] = src[i, 32:64, 0:12].reshape(768, 128)
        x2[:, 0] = pick(t, v).astype(BF16).reshape(32, 6, 2, 128)
        x2[:, 1] = pltpu.roll(pick(v, t), 64, 1).astype(BF16).reshape(32, 6, 2, 128)
        xs[i, :, 256:384] = x2[...].reshape(768, 128)

    def core_copy(src, dst, i):
        return pltpu.make_async_remote_copy(
            src_ref=src, dst_ref=dst, send_sem=core_send.at[i], recv_sem=core_recv.at[i],
            device_id=sibling, device_id_type=MESH,
        )

    def mix_out():
        for ab in range(2):
            build(left_right0, ab * 2 + 1)
        copies = [core_copy(xs.at[ab * 2 + 1], xr.at[ab], ab) for ab in range(2)]
        for copy in copies:
            copy.start()
        for ab in range(2):
            build(left_right0, ab * 2)

        def contract(ab, right, owner):
            got = lax.dot_general(right, xs[ab * 2], (((0,), (0,)), ((), ())), preferred_element_type=F32)
            for it in range(3):
                at = it * 1536 + ab
                piece = got[:, it * 128:(it + 1) * 128]
                work[pl.ds(at + owner * 384, 128, stride=2), :] = piece[0:128]
                work[pl.ds(at + owner * 384 + 768, 128, stride=2), :] = piece[128:256]
                work[pl.ds(at + owner * 384 + 256, 64, stride=2), :] = piece[256:320]
                work[pl.ds(at + owner * 384 + 1024, 64, stride=2), :] = piece[320:384]

        for ab in range(2):
            contract(ab, xs[ab * 2 + 1], core)
        for ab in range(2):
            copies[ab].wait()
            contract(ab, xr[ab], 1 - core)

    def mix_in():
        for i in range(4):
            build(left_right1, i)

        def contract(ab, owner):
            first = pl.multiple_of(owner * 192, 64)
            i = ab * 2
            left = jnp.concatenate(
                [
                    xs[i, pl.ds(first, 128), :],
                    xs[i, pl.ds(first + 384, 128), :],
                    xs[i, pl.ds(first + 128, 64), :],
                    xs[i, pl.ds(first + 512, 64), :],
                ],
                0,
            )
            return lax.dot_general(xs[i + 1], left, (((1,), (1,)), ((), ())), preferred_element_type=F32)

        copies = []
        for ab in range(2):
            got = contract(ab, 1 - core)
            for it in range(3):
                part_out[ab, it] = got[:, it * 128:(it + 1) * 128].astype(BF16)
            copies.append(core_copy(part_out.at[ab], part_in.at[ab], 2 + ab))
            copies[ab].start()
        for ab in range(2):
            got = contract(ab, core)
            for it in range(3):
                part_own[ab, it] = got[:, it * 128:(it + 1) * 128]
        for ab in range(2):
            copies[ab].wait()
            for it in range(3):
                work[pl.ds(it * 1536 + ab, 768, stride=2), :] = part_own[ab, it] + part_in[ab, it].astype(F32)

    def pack():
        for it in range(2):
            rows = work[it * 1536:(it + 1) * 1536].astype(BF16)
            ret[it * 32:(it + 1) * 32, 0:24] = rows.reshape(32, 24, 2, 128)

        @pl.loop(0, 32)
        def _(q):
            first = pl.multiple_of(3072 + 48 * q, 8)
            top = work[pl.ds(first, 24), :]
            bot = pltpu.roll(work[pl.ds(first + 24, 24), :], 64, 1)
            ret[q, 24:36] = pick(top, bot).astype(BF16).reshape(12, 2, 128)
            ret[32 + q, 24:36] = pick(bot, top).astype(BF16).reshape(12, 2, 128)

    def finish(p, mix, u):
        cols = []
        for e in range(2):
            halves = []
            for h in range(2):
                vals = mix[2 * (2 * u + e) + h].reshape(128, 128).astype(F32)
                halves.append(norm_cols(vals, gain_out[p]).astype(BF16))
            cols.append(jnp.concatenate(halves, 0))
        got = jnp.dot(out_a[p], jnp.concatenate(cols, 1), preferred_element_type=F32)
        for e in range(2):
            tp = 2 * u + e
            zt[tp] = (zt[tp].astype(F32) + gate[tp] * got[:, e * 128:(e + 1) * 128]).astype(BF16)

    @pl.loop(0, 9)
    def _(u):
        project(0, u)

    pl.semaphore_wait(barrier, CHIPS)

    for p in range(2):
        arrived, mixed = ((left_right0, mix0), (left_right1, mix1))[p]
        send_all(lambda d: msg.at[:, :, d], arrived.at[:, me], fwd_send.at[p], fwd_recv.at[p])
        gates(p)
        wait_bytes(arrived, fwd_recv.at[p])
        (mix_out, mix_in)[p]()
        pack()
        send_all(lambda d: ret.at[d], mixed.at[:, me], ret_send.at[p], ret_recv.at[p])
        wait_bytes(msg.at[:, :, pl.ds(0, CHIPS - 1)], fwd_send.at[p])
        wait_bytes(mixed, ret_recv.at[p])
        wait_bytes(ret.at[pl.ds(0, CHIPS - 1)], ret_send.at[p])

        @pl.loop(0, 9)
        def _(u):
            finish(p, mixed, u)
            if p == 0:
                project(1, u)

    @pl.loop(0, 12)
    def _(tp):
        for e in range(2):
            work[pl.ds(2 * tp + e, 128, stride=24), :] = zt[tp, e * 128:(e + 1) * 128].astype(F32).T

    @pl.loop(0, 6)
    def _(tp):
        for e in range(2):
            m = 2 * tp + e
            vals = zt[12 + tp, e * 128:(e + 1) * 128].astype(F32).T
            work[pl.ds(128 * 24 + m + 12 * y_hi, 64, stride=24), :] = vals[0:64]
            work[pl.ds(128 * 24 + m + 12 * (1 - y_hi), 64, stride=24), :] = vals[64:128]

    out[...] = work[...].astype(BF16)


def on_device(pair, norm_in, proj_weight, gate_weight, norm_out, out_weight):
    vmem = pl.BlockSpec(memory_space=pltpu.VMEM)
    updated = pl.pallas_call(
        kernel,
        out_shape=jax.ShapeDtypeStruct((ROWS * COLS, C), BF16),
        in_specs=[vmem] * 6,
        out_specs=vmem,
        scratch_shapes=[
            pltpu.VMEM((PAIRS, 256, 128), BF16),
            pltpu.VMEM((PAIRS, 256, 128), BF16),
            pltpu.VMEM((PAIRS, 256, 128), F32),
            pltpu.VMEM((4, PAIRS, CHIPS, 2, 128), BF16),
            pltpu.VMEM((4, CHIPS, PAIRS, 2, 128), BF16),
            pltpu.VMEM((4, CHIPS, PAIRS, 2, 128), BF16),
            pltpu.VMEM((4, TOKENS, 384), BF16),
            pltpu.VMEM((2, TOKENS, 384), BF16),
            pltpu.VMEM((2, 3, TOKENS, 128), BF16),
            pltpu.VMEM((2, 3, TOKENS, 128), BF16),
            pltpu.VMEM((2, 3, TOKENS, 128), F32),
            pltpu.VMEM((CHIPS, 36, 2, 128), BF16),
            pltpu.VMEM((36, CHIPS, 2, 128), BF16),
            pltpu.VMEM((36, CHIPS, 2, 128), BF16),
            pltpu.VMEM((ROWS * COLS, 128), F32),
            pltpu.VMEM((1024, 128), F32),
            pltpu.VMEM((1024, 128), F32),
            pltpu.VMEM((2, 1024, 256), BF16),
            pltpu.VMEM((2, 256, 256), BF16),
            pltpu.VMEM((2, 256, 256), BF16),
            pltpu.VMEM((2, 128, 128), F32),
            pltpu.VMEM((2, 128, 128), F32),
            pltpu.VMEM((32, 2, 6, 2, 128), BF16),
        ] + [pltpu.SemaphoreType.DMA((2,))] * 4 + [pltpu.SemaphoreType.DMA((4,))] * 2,
        compiler_params=pltpu.CompilerParams(
            collective_id=0, has_side_effects=True, vmem_limit_bytes=56 * 2**20
        ),
    )(pair.reshape(ROWS * COLS, C), norm_in, proj_weight, gate_weight, norm_out, out_weight)
    return updated.reshape(ROWS, COLS, C)


def solution(mesh):
    placed = (P("row", "col", None), P(), P(), P(), P(), P())
    return jax.shard_map(
        on_device, mesh=mesh, in_specs=placed, out_specs=P("row", "col", None), check_vma=False
    )
```

profile of v0, /device:TPU:1, one launch (start us, length us, event | category | flops | bytes accessed | tf_op | source)
XLA Modules:
  0.0 145.1 jit_solution(14820819588859337561)
XLA Ops:
  0.0 142.6 %shard_map.64 = bf16[4608,128]{1,0:T(8,128)(2,1)} custom-call(bf16[4608,128]{1,0:T(8,128)(2,1)} %bitcast.3, f32[2,128]{1,0:T(2,128)} %norm_in.1, bf16[2,128,512]{2,1,0:T(8,128)(2,1)} %proj_w.1, bf16[2,128,128]{2,1,0:T(8,128)(2,1)} %gate_w.1, f32[2,128]{1,0:T(2,128)} %norm_out.1, bf16[2,128,128]{2,1,0:T(8,128)(2,1)} %out_w.1), custom_call_target="tpu_custom_call" | custom-call | tf_op jit(solution)/shard_map/pallas_call | solution.py:283
  142.6 2.5 %copy.8 = bf16[192,24,128]{2,1,0:T(8,128)(2,1)} copy(bf16[192,24,128]{2,1,0:T(8,128)(2,1)} %bitcast.2) | data formatting | bytes 2359296
where the time goes:
time: 145 us
  Pallas kernels  143 us (99%)
  local copies, waits for them, and re-layouts  2.49 us (2%)
    pallas_call x1, Pallas kernels, on_device(): pl.pallas_call(kernel, out_shape=jax.ShapeDtypeStruct((ROWS * COLS, C), B...  143 us

commit v1 on v0

v1 whole, which is shorter than its diff:
```python
import functools

import jax
import jax.numpy as jnp
from jax import lax
from jax.experimental import pallas as pl
from jax.experimental.pallas import tpu as pltpu
from jax.sharding import PartitionSpec as P

F32, BF16 = jnp.float32, jnp.bfloat16
MESH = pl.DeviceIdType.MESH

ROWS, COLS, C = 192, 24, 128
CHIPS = 64
PAIRS = 18
TOKENS = 768


def chip_coords():
    row, col = lax.axis_index("row"), lax.axis_index("col")
    return col // 8, (row // 2) * 2 + col % 2, (col // 2) % 4, row % 2


def norm_cols(values, gain):
    mean = jnp.mean(values, 0, keepdims=True)
    centered = values - mean
    variance = jnp.mean(centered * centered, 0, keepdims=True)
    return centered * lax.rsqrt(variance + 1e-05) * gain


def sigmoid(values):
    return 0.5 * jnp.tanh(0.5 * values) + 0.5


def kernel(
    pair, norm_in, proj_w, gate_w, norm_out, out_w, out,
    pbuf, zt, nb, gate, msg, left_right0, left_right1, xl0, xt0, xt0_far, xl1, xr1, xl1_far, xr1_far, acc, ret, mix0, mix1,
    work, wfa, wfb, proj_a, gate_a, out_a, gain_in, gain_out, x2,
    fwd_send, fwd_recv, ret_send, ret_recv, core_send, core_recv, local,
):
    x, y, z, core = chip_coords()
    y_hi = y // 2
    col = lax.axis_index("col")
    me = y_hi * 32 + col
    sibling = (y_hi * 2 + 1 - core, col)
    y_of = [lax.rem(y + b, 4) for b in range(4)]
    row_of = [v // 2 for v in y_of]
    low_of = [lax.rem(v, 2) for v in y_of]
    z_of = [lax.rem(z + c, 4) * 2 for c in range(4)]

    def pick(a, b):
        return jnp.where(lax.broadcasted_iota(jnp.int32, a.shape, 1) < 64, a, b)

    def each_peer(act):
        @pl.loop(0, 4)
        def _(i):
            for n in range(16):
                b, c = n % 4, (n // 4 + n) % 4
                px = lax.rem(x + (b + c) % 4 + i, 4) * 8

                def one():
                    act(row_of[b], px + low_of[b] + z_of[c])

                if n == 0:
                    pl.when(i > 0)(one)
                else:
                    one()

    def send_all(src_of, dst, send, recv):
        def one(py, pc):
            pltpu.make_async_remote_copy(
                src_ref=src_of(py * 32 + pc), dst_ref=dst, send_sem=send, recv_sem=recv,
                device_id=(py * 2 + core, pc), device_id_type=MESH,
            ).start()

        each_peer(one)
        pltpu.make_async_copy(src_of(me), dst, recv).start()

    def wait_bytes(ref, sem):
        pltpu.make_async_copy(ref, ref, sem).wait()

    loads = [
        pltpu.make_async_copy(pair.at[pl.ds(a, n)], pbuf.at[pl.ds(a, n)], local.at[i])
        for i, (a, n) in enumerate(((0, 3072), (3072, 1536)))
    ]
    for load in loads:
        load.start()

    barrier = pltpu.get_barrier_semaphore()
    pl.semaphore_signal(barrier, inc=1, device_id=sibling, device_id_type=MESH)
    each_peer(lambda py, pc: pl.semaphore_signal(
        barrier, inc=1, device_id=(py * 2 + core, pc), device_id_type=MESH))

    def picked_gain(ref, p):
        rows = lax.broadcasted_iota(jnp.int32, (2, 128), 0) == p
        row = jnp.sum(jnp.where(rows, ref[...], 0.0), 0, keepdims=True)
        return jnp.broadcast_to(row, (128, 128)).T

    def prepare_in(p):
        wt = proj_w[p].astype(F32).T
        wfa[pl.ds(0, 512, stride=2), :] = wt
        wfa[pl.ds(1, 512, stride=2), :] = jnp.zeros_like(wt)
        wfb[pl.ds(0, 512, stride=2), :] = jnp.zeros_like(wt)
        wfb[pl.ds(1, 512, stride=2), :] = wt
        proj_a[p, :, 0:128] = wfa[...].astype(BF16)
        proj_a[p, :, 128:256] = wfb[...].astype(BF16)
        gain_in[p] = picked_gain(norm_in, p)

    def prepare_out(p):
        gt = gate_w[p].astype(F32).T.astype(BF16)
        wfa[pl.ds(0, 64, stride=2), :] = out_w[p, 0:64].astype(F32)
        wfa[pl.ds(1, 64, stride=2), :] = out_w[p, 64:128].astype(F32)
        ot = wfa[0:128].T.astype(BF16)
        zero = jnp.zeros((128, 128), BF16)
        for dst, block in ((gate_a, gt), (out_a, ot)):
            dst[p, 0:128, 0:128] = block
            dst[p, 0:128, 128:256] = zero
            dst[p, 128:256, 0:128] = zero
            dst[p, 128:256, 128:256] = block
        gain = picked_gain(norm_out, p)
        wfa[pl.ds(0, 64, stride=2), :] = gain[0:64]
        wfa[pl.ds(1, 64, stride=2), :] = gain[64:128]
        gain_out[p] = wfa[0:128]

    def half_rows(m, first):
        return pl.ds(128 * 24 + m + 12 * first, 64, stride=24)

    def load_tiles(tp, mixed):
        for e in range(2):
            if mixed:
                m = 2 * tp + e - 24
                vals = jnp.concatenate([work[half_rows(m, y_hi), :], work[half_rows(m, 1 - y_hi), :]], 0)
            else:
                vals = work[pl.ds(2 * tp + e, 128, stride=24), :]
            zt[tp, e * 128:(e + 1) * 128] = vals.T.astype(BF16)

    def store_tiles(tp, mixed):
        for e in range(2):
            vals = zt[tp, e * 128:(e + 1) * 128].astype(F32).T
            if mixed:
                m = 2 * tp + e - 24
                work[half_rows(m, y_hi), :] = vals[0:64]
                work[half_rows(m, 1 - y_hi), :] = vals[64:128]
            else:
                work[pl.ds(2 * tp + e, 128, stride=24), :] = vals

    def project(p, u):
        for e in range(2):
            tp = 2 * u + e
            for h in range(2):
                rows = slice(h * 128, (h + 1) * 128)
                nb[tp, rows] = norm_cols(zt[tp, rows].astype(F32), gain_in[p]).astype(BF16)
        n = jnp.concatenate([nb[2 * u], nb[2 * u + 1]], 1)
        for side in range(2):
            a = proj_a[p, side * 512:(side + 1) * 512]
            got = jnp.dot(a, n, preferred_element_type=F32)
            val = (sigmoid(got[256:512]) * got[0:256]).astype(BF16)
            for ab in range(2):
                for e in range(2):
                    block = val[ab * 128:(ab + 1) * 128, e * 128:(e + 1) * 128]
                    msg[ab * 2 + side, 2 * u + e] = block.reshape(64, 2, 128)

    def gates(p):
        @pl.loop(0, 9)
        def _(u):
            n = jnp.concatenate([nb[2 * u], nb[2 * u + 1]], 1)
            g = sigmoid(jnp.dot(gate_a[p], n, preferred_element_type=F32))
            gate[2 * u] = g[:, 0:128]
            gate[2 * u + 1] = g[:, 128:256]

    def send_group(p, g):
        arrived = (left_right0, left_right1)[p]
        send_all(
            lambda d: msg.at[:, pl.ds(6 * g, 6), d], arrived.at[:, me, pl.ds(6 * g, 6)],
            fwd_send.at[p, g], fwd_recv.at[p, g],
        )

    def wait_group(p, g):
        arrived = (left_right0, left_right1)[p]
        wait_bytes(arrived.at[:, :, pl.ds(6 * g, 6)], fwd_recv.at[p, g])

    def wait_group_sent(p, g):
        wait_bytes(msg.at[:, pl.ds(6 * g, 6), pl.ds(0, CHIPS - 1)], fwd_send.at[p, g])

    def main_cols(src, i, it):
        return src[i, 32 * it:32 * (it + 1), 0:12].reshape(768, 128)

    def mixed_cols(src, i):
        t = src[i, 0:32, 12:18].reshape(384, 128).astype(F32)
        v = src[i, 32:64, 12:18].reshape(384, 128).astype(F32)
        x2[:, 0] = pick(t, v).astype(BF16).reshape(32, 6, 2, 128)
        x2[:, 1] = pltpu.roll(pick(v, t), 64, 1).astype(BF16).reshape(32, 6, 2, 128)
        return x2[...].reshape(768, 128)

    def core_copy(src, dst, i):
        return pltpu.make_async_remote_copy(
            src_ref=src, dst_ref=dst, send_sem=core_send.at[i], recv_sem=core_recv.at[i],
            device_id=sibling, device_id_type=MESH,
        )

    def place(ab, got, first_it, jt, owner):
        for n in range(got.shape[1] // 128):
            at = (first_it + n) * 1536 + ab + owner * 384
            piece = got[:, n * 128:(n + 1) * 128]
            if jt < 2:
                work[pl.ds(at + 768 * jt, 128, stride=2), :] = piece
            else:
                work[pl.ds(at + 256, 64, stride=2), :] = piece[0:64]
                work[pl.ds(at + 1024, 64, stride=2), :] = piece[64:128]

    def mix_out():
        src = left_right0
        wait_group(0, 0)
        wait_group(0, 1)
        for ab in range(2):
            for it in range(2):
                xt0[ab, it * 128:(it + 1) * 128] = main_cols(src, ab * 2 + 1, it).T
        main = core_copy(xt0.at[:, pl.ds(0, 256)], xt0_far.at[:, pl.ds(0, 256)], 0)
        main.start()
        for ab in range(2):
            for it in range(2):
                xl0[ab, :, it * 128:(it + 1) * 128] = main_cols(src, ab * 2, it)

        def contract(right, jt, cols, owner):
            for ab in range(2):
                r = right[ab, jt * 128:(jt + 1) * 128]
                got = jnp.dot(r, xl0[ab, :, cols], preferred_element_type=F32)
                place(ab, got, cols.start // 128, jt, owner)

        for jt in range(2):
            contract(xt0, jt, slice(0, 256), core)
        main.wait()
        for jt in range(2):
            contract(xt0_far, jt, slice(0, 256), 1 - core)

        wait_group(0, 2)
        for ab in range(2):
            xt0[ab, 256:384] = mixed_cols(src, ab * 2 + 1).T
        mixed = core_copy(xt0.at[:, pl.ds(256, 128)], xt0_far.at[:, pl.ds(256, 128)], 1)
        mixed.start()
        for ab in range(2):
            xl0[ab, :, 256:384] = mixed_cols(src, ab * 2)
        contract(xt0, 2, slice(0, 384), core)
        for jt in range(2):
            contract(xt0, jt, slice(256, 384), core)
            contract(xt0_far, jt, slice(256, 384), 1 - core)
        mixed.wait()
        contract(xt0_far, 2, slice(0, 384), 1 - core)

    def own_rows(ref):
        return jnp.concatenate([ref[0, 0:128], ref[1, 0:128], ref[0, 128:192], ref[1, 128:192]], 0)

    def mix_in():
        src = left_right1

        def exchange(cols, i):
            right = core_copy(xr1.at[:, :, cols], xr1_far.at[:, :, cols], i)
            left = core_copy(xl1.at[:, :, 1 - core, :, cols], xl1_far.at[:, :, :, cols], i + 1)
            right.start()
            left.start()
            return right, left

        def contract(ab, cols):
            right = jnp.concatenate([xr1[ab, :, cols], xr1_far[ab, :, cols]], 1)
            own = own_rows(xl1.at[ab, :, core, :, cols])
            far = own_rows(xl1_far.at[ab, :, :, cols])
            left = jnp.concatenate([own, far], 1)
            return lax.dot_general(right, left, (((1,), (1,)), ((), ())), preferred_element_type=F32)

        wait_group(1, 0)
        wait_group(1, 1)
        for ab in range(2):
            for it in range(2):
                xr1[ab, :, it * 128:(it + 1) * 128] = main_cols(src, ab * 2 + 1, it)
                xl1[ab, :, :, :, it * 128:(it + 1) * 128] = main_cols(src, ab * 2, it).reshape(2, 2, 192, 128)
        copies = exchange(pl.ds(0, 256), 2)
        for copy in copies:
            copy.wait()
        for ab in range(2):
            acc[ab] = contract(ab, pl.ds(0, 256))

        wait_group(1, 2)
        for ab in range(2):
            xr1[ab, :, 256:384] = mixed_cols(src, ab * 2 + 1)
            xl1[ab, :, :, :, 256:384] = mixed_cols(src, ab * 2).reshape(2, 2, 192, 128)
        copies = exchange(pl.ds(256, 128), 4)
        for copy in copies:
            copy.wait()
        for ab in range(2):
            got = contract(ab, pl.ds(256, 128)) + acc[ab]
            for it in range(3):
                work[pl.ds(it * 1536 + ab, 768, stride=2), :] = got[:, it * 128:(it + 1) * 128]

    def give_back(p):
        mixed = (mix0, mix1)[p]
        for it in range(2):
            rows = work[it * 1536:(it + 1) * 1536].astype(BF16)
            ret[it * 32:(it + 1) * 32, 0:24] = rows.reshape(32, 24, 2, 128)
        send_all(lambda d: ret.at[d, pl.ds(0, 24)], mixed.at[pl.ds(0, 24), me], ret_send.at[p, 0], ret_recv.at[p, 0])

        @pl.loop(0, 32)
        def _(q):
            first = pl.multiple_of(3072 + 48 * q, 8)
            top = work[pl.ds(first, 24), :]
            bot = pltpu.roll(work[pl.ds(first + 24, 24), :], 64, 1)
            ret[q, 24:36] = pick(top, bot).astype(BF16).reshape(12, 2, 128)
            ret[32 + q, 24:36] = pick(bot, top).astype(BF16).reshape(12, 2, 128)

        send_all(lambda d: ret.at[d, pl.ds(24, 12)], mixed.at[pl.ds(24, 12), me], ret_send.at[p, 1], ret_recv.at[p, 1])

    def wait_back(p, part):
        rows = ((0, 24), (24, 12))[part]
        wait_bytes((mix0, mix1)[p].at[pl.ds(*rows)], ret_recv.at[p, part])

    def wait_back_sent(p):
        for part, rows in enumerate(((0, 24), (24, 12))):
            wait_bytes(ret.at[pl.ds(0, CHIPS - 1), pl.ds(*rows)], ret_send.at[p, part])

    def finish(p, u):
        mix = (mix0, mix1)[p]
        cols = []
        for e in range(2):
            halves = []
            for h in range(2):
                vals = mix[2 * (2 * u + e) + h].reshape(128, 128).astype(F32)
                halves.append(norm_cols(vals, gain_out[p]).astype(BF16))
            cols.append(jnp.concatenate(halves, 0))
        got = jnp.dot(out_a[p], jnp.concatenate(cols, 1), preferred_element_type=F32)
        for e in range(2):
            tp = 2 * u + e
            zt[tp] = (zt[tp].astype(F32) + gate[tp] * got[:, e * 128:(e + 1) * 128]).astype(BF16)

    prepare_in(0)
    for g in range(3):
        if g == 0:
            loads[0].wait()
            work[0:3072] = pbuf[0:3072].astype(F32)
        if g == 2:
            loads[1].wait()
            work[3072:4608] = pbuf[3072:4608].astype(F32)

        @pl.loop(3 * g, 3 * g + 3)
        def _(u):
            for e in range(2):
                load_tiles(2 * u + e, g == 2)
            project(0, u)

        if g == 0:
            pl.semaphore_wait(barrier, CHIPS)
        send_group(0, g)

    prepare_out(0)
    gates(0)
    prepare_in(1)
    prepare_out(1)
    mix_out()
    give_back(0)
    for g in range(3):
        wait_group_sent(0, g)
    for g in range(3):
        if g != 1:
            wait_back(0, g // 2)

        @pl.loop(3 * g, 3 * g + 3)
        def _(u):
            finish(0, u)
            project(1, u)

        send_group(1, g)

    gates(1)
    wait_back_sent(0)
    mix_in()
    give_back(1)
    for g in range(3):
        wait_group_sent(1, g)
    stores = [
        pltpu.make_async_copy(pbuf.at[pl.ds(a, n)], out.at[pl.ds(a, n)], local.at[2 + i])
        for i, (a, n) in enumerate(((0, 3072), (3072, 1536)))
    ]
    for part, (first, last) in enumerate(((0, 6), (6, 9))):
        wait_back(1, part)

        @pl.loop(first, last)
        def _(u):
            finish(1, u)
            for e in range(2):
                store_tiles(2 * u + e, part == 1)

        rows = ((0, 3072), (3072, 4608))[part]
        pbuf[rows[0]:rows[1]] = work[rows[0]:rows[1]].astype(BF16)
        stores[part].start()
    wait_back_sent(1)
    for store in stores:
        store.wait()


def on_device(pair, norm_in, proj_weight, gate_weight, norm_out, out_weight):
    vmem = pl.BlockSpec(memory_space=pltpu.VMEM)
    hbm = pl.BlockSpec(memory_space=pl.ANY)
    updated = pl.pallas_call(
        kernel,
        out_shape=jax.ShapeDtypeStruct((ROWS * COLS, C), BF16),
        in_specs=[hbm] + [vmem] * 5,
        out_specs=hbm,
        scratch_shapes=[
            pltpu.VMEM((ROWS * COLS, C), BF16),
            pltpu.VMEM((PAIRS, 256, 128), BF16),
            pltpu.VMEM((PAIRS, 256, 128), BF16),
            pltpu.VMEM((PAIRS, 256, 128), F32),
            pltpu.VMEM((4, PAIRS, CHIPS, 2, 128), BF16),
            pltpu.VMEM((4, CHIPS, PAIRS, 2, 128), BF16),
            pltpu.VMEM((4, CHIPS, PAIRS, 2, 128), BF16),
            pltpu.VMEM((2, TOKENS, 384), BF16),
            pltpu.VMEM((2, 384, TOKENS), BF16),
            pltpu.VMEM((2, 384, TOKENS), BF16),
            pltpu.VMEM((2, 2, 2, 192, 384), BF16),
            pltpu.VMEM((2, TOKENS, 384), BF16),
            pltpu.VMEM((2, 2, 192, 384), BF16),
            pltpu.VMEM((2, TOKENS, 384), BF16),
            pltpu.VMEM((2, TOKENS, 384), F32),
            pltpu.VMEM((CHIPS, 36, 2, 128), BF16),
            pltpu.VMEM((36, CHIPS, 2, 128), BF16),
            pltpu.VMEM((36, CHIPS, 2, 128), BF16),
            pltpu.VMEM((ROWS * COLS, 128), F32),
            pltpu.VMEM((1024, 128), F32),
            pltpu.VMEM((1024, 128), F32),
            pltpu.VMEM((2, 1024, 256), BF16),
            pltpu.VMEM((2, 256, 256), BF16),
            pltpu.VMEM((2, 256, 256), BF16),
            pltpu.VMEM((2, 128, 128), F32),
            pltpu.VMEM((2, 128, 128), F32),
            pltpu.VMEM((32, 2, 6, 2, 128), BF16),
            pltpu.SemaphoreType.DMA((2, 3)),
            pltpu.SemaphoreType.DMA((2, 3)),
            pltpu.SemaphoreType.DMA((2, 2)),
            pltpu.SemaphoreType.DMA((2, 2)),
            pltpu.SemaphoreType.DMA((6,)),
            pltpu.SemaphoreType.DMA((6,)),
            pltpu.SemaphoreType.DMA((4,)),
        ],
        compiler_params=pltpu.CompilerParams(
            collective_id=0, has_side_effects=True, vmem_limit_bytes=56 * 2**20
        ),
    )(pair.reshape(ROWS * COLS, C), norm_in, proj_weight, gate_weight, norm_out, out_weight)
    return updated.reshape(ROWS, COLS, C)


def solution(mesh):
    placed = (P("row", "col", None), P(), P(), P(), P(), P())
    return jax.shard_map(
        on_device, mesh=mesh, in_specs=placed, out_specs=P("row", "col", None), check_vma=False
    )
```

time: 145 us -> 117 us (0.81)
  Pallas kernels: 143 us -> 114 us
    pallas_call x1, Pallas kernels: 143 us -> 114 us  [on_device(): pl.pallas_call(kernel, out_shape=jax.ShapeDtypeStruct((ROWS * COLS, C), B...]
where the time goes in v1:
time: 117 us
  Pallas kernels  114 us (97%)
  local copies, waits for them, and re-layouts  2.49 us (2%)
    pallas_call x1, Pallas kernels, on_device(): pl.pallas_call(kernel, out_shape=jax.ShapeDtypeStruct((ROWS * COLS, C), B...  114 us
    unnamed x1, local copies, waits for them, and re-layouts  2.49 us

profile of v1, /device:TPU:1, one launch (start us, length us, event | category | flops | bytes accessed | tf_op | source)
XLA Modules:
  0.0 116.7 jit_solution(11176938144077946230)
XLA Ops:
  0.0 114.2 %shard_map.64 = bf16[4608,128]{1,0:T(8,128)(2,1)} custom-call(bf16[4608,128]{1,0:T(8,128)(2,1)} %bitcast.3, f32[2,128]{1,0:T(2,128)} %norm_in.1, bf16[2,128,512]{2,1,0:T(8,128)(2,1)} %proj_w.1, bf16[2,128,128]{2,1,0:T(8,128)(2,1)} %gate_w.1, f32[2,128]{1,0:T(2,128)} %norm_out.1, bf16[2,128,128]{2,1,0:T(8,128)(2,1)} %out_w.1), custom_call_target="tpu_custom_call" | custom-call | tf_op jit(solution)/shard_map/pallas_call | solution.py:401
  114.2 2.5 %copy.8 = bf16[192,24,128]{2,1,0:T(8,128)(2,1)} copy(bf16[192,24,128]{2,1,0:T(8,128)(2,1)} %bitcast.2) | data formatting | bytes 2359296

commit v2 on v1

v2 whole, which is shorter than its diff:
```python
import functools

import jax
import jax.numpy as jnp
from jax import lax
from jax.experimental import pallas as pl
from jax.experimental.pallas import tpu as pltpu
from jax.sharding import PartitionSpec as P

F32, BF16 = jnp.float32, jnp.bfloat16
MESH = pl.DeviceIdType.MESH

ROWS, COLS, C = 192, 24, 128
CHIPS = 64
PAIRS = 18
THIRDS = ((0, 6), (6, 6), (12, 6))
FWD = ((((0, 18),), ((0, 18),)), (THIRDS, ((0, 18),)))
RET = ((((0, 18),), THIRDS), (((0, 18),), THIRDS))
TOKENS = 768


def chip_coords():
    row, col = lax.axis_index("row"), lax.axis_index("col")
    return col // 8, (row // 2) * 2 + col % 2, (col // 2) % 4, row % 2


def norm_cols(values, gain):
    mean = jnp.mean(values, 0, keepdims=True)
    centered = values - mean
    variance = jnp.mean(centered * centered, 0, keepdims=True)
    return centered * lax.rsqrt(variance + 1e-05) * gain


def sigmoid(values):
    return 0.5 * jnp.tanh(0.5 * values) + 0.5


def kernel(
    pair, norm_in, proj_w, gate_w, norm_out, out_w, out,
    pbuf, zt, nb, gate, msg, left_right0, left_right1, xl0, xt0, xt0_far, xl1, xr1, xl1_far, xr1_far, mixed, ret, mix0, mix1,
    work, wfa, wfb, proj_a, gate_a, out_a, gain_in, gain_out, x2,
    fwd_send, fwd_recv, ret_send, ret_recv, core_send, core_recv, local,
):
    x, y, z, core = chip_coords()
    y_hi = y // 2
    col = lax.axis_index("col")
    me = y_hi * 32 + col
    sibling = (y_hi * 2 + 1 - core, col)
    y_of = [lax.rem(y + b, 4) for b in range(4)]
    row_of = [v // 2 for v in y_of]
    low_of = [lax.rem(v, 2) for v in y_of]
    z_of = [lax.rem(z + c, 4) * 2 for c in range(4)]

    def pick(a, b):
        return jnp.where(lax.broadcasted_iota(jnp.int32, a.shape, 1) < 64, a, b)

    def each_peer(act):
        @pl.loop(0, 4)
        def _(i):
            for n in range(16):
                b, c = n % 4, (n // 4 + n) % 4
                px = lax.rem(x + (b + c) % 4 + i, 4) * 8

                def one():
                    act(row_of[b], px + low_of[b] + z_of[c])

                if n == 0:
                    pl.when(i > 0)(one)
                else:
                    one()

    def send_all(src_of, dst, send, recv):
        def one(py, pc):
            pltpu.make_async_remote_copy(
                src_ref=src_of(py * 32 + pc), dst_ref=dst, send_sem=send, recv_sem=recv,
                device_id=(py * 2 + core, pc), device_id_type=MESH,
            ).start()

        each_peer(one)
        pltpu.make_async_copy(src_of(me), dst, recv).start()

    def wait_bytes(ref, sem):
        pltpu.make_async_copy(ref, ref, sem).wait()

    loads = [
        pltpu.make_async_copy(pair.at[pl.ds(a, n)], pbuf.at[pl.ds(a, n)], local.at[i])
        for i, (a, n) in enumerate(((0, 3072), (3072, 1536)))
    ]
    for load in loads:
        load.start()

    barrier = pltpu.get_barrier_semaphore()
    pl.semaphore_signal(barrier, inc=1, device_id=sibling, device_id_type=MESH)
    each_peer(lambda py, pc: pl.semaphore_signal(
        barrier, inc=1, device_id=(py * 2 + core, pc), device_id_type=MESH))

    def picked_gain(ref, p):
        rows = lax.broadcasted_iota(jnp.int32, (2, 128), 0) == p
        row = jnp.sum(jnp.where(rows, ref[...], 0.0), 0, keepdims=True)
        return jnp.broadcast_to(row, (128, 128)).T

    def prepare_in(p):
        wt = proj_w[p].astype(F32).T
        wfa[pl.ds(0, 512, stride=2), :] = wt
        wfa[pl.ds(1, 512, stride=2), :] = jnp.zeros_like(wt)
        wfb[pl.ds(0, 512, stride=2), :] = jnp.zeros_like(wt)
        wfb[pl.ds(1, 512, stride=2), :] = wt
        proj_a[p, :, 0:128] = wfa[...].astype(BF16)
        proj_a[p, :, 128:256] = wfb[...].astype(BF16)
        gain_in[p] = picked_gain(norm_in, p)

    def prepare_out(p):
        gt = gate_w[p].astype(F32).T.astype(BF16)
        zero = jnp.zeros((128, 128), BF16)
        gate_a[p, 0:128, 0:128] = gt
        gate_a[p, 0:128, 128:256] = zero
        gate_a[p, 128:256, 0:128] = zero
        gate_a[p, 128:256, 128:256] = gt
        ow = out_w[p].astype(F32)
        for e in range(2):
            wfa[pl.ds(e, 128, stride=2), :] = ow
            wfa[pl.ds(1 - e, 128, stride=2), :] = jnp.zeros_like(ow)
            out_a[p, e * 128:(e + 1) * 128] = wfa[0:256].T.astype(BF16)
        gain = picked_gain(norm_out, p)
        for e in range(2):
            wfa[pl.ds(e, 128, stride=2), :] = gain
        gain_out[p] = wfa[0:256]

    def half_rows(m, first):
        return pl.ds(128 * 24 + m + 12 * first, 64, stride=24)

    def load_tiles(tp, mixed):
        for e in range(2):
            if mixed:
                m = 2 * tp + e - 24
                vals = jnp.concatenate([work[half_rows(m, y_hi), :], work[half_rows(m, 1 - y_hi), :]], 0)
            else:
                vals = work[pl.ds(2 * tp + e, 128, stride=24), :]
            zt[tp, e * 128:(e + 1) * 128] = vals.T.astype(BF16)

    def store_tiles(tp, mixed):
        for e in range(2):
            vals = zt[tp, e * 128:(e + 1) * 128].astype(F32).T
            if mixed:
                m = 2 * tp + e - 24
                work[half_rows(m, y_hi), :] = vals[0:64]
                work[half_rows(m, 1 - y_hi), :] = vals[64:128]
            else:
                work[pl.ds(2 * tp + e, 128, stride=24), :] = vals

    def project(p, u):
        for e in range(2):
            tp = 2 * u + e
            for h in range(2):
                rows = slice(h * 128, (h + 1) * 128)
                nb[tp, rows] = norm_cols(zt[tp, rows].astype(F32), gain_in[p]).astype(BF16)
        n = jnp.concatenate([nb[2 * u], nb[2 * u + 1]], 1)
        for side in range(2):
            a = proj_a[p, side * 512:(side + 1) * 512]
            got = jnp.dot(a, n, preferred_element_type=F32)
            val = (sigmoid(got[256:512]) * got[0:256]).astype(BF16)
            for ab in range(2):
                for e in range(2):
                    block = val[ab * 128:(ab + 1) * 128, e * 128:(e + 1) * 128]
                    msg[ab * 2 + side, 2 * u + e] = block.reshape(64, 2, 128)

    def gates(p):
        @pl.loop(0, 9)
        def _(u):
            n = jnp.concatenate([nb[2 * u], nb[2 * u + 1]], 1)
            g = sigmoid(jnp.dot(gate_a[p], n, preferred_element_type=F32))
            gate[2 * u] = g[:, 0:128]
            gate[2 * u + 1] = g[:, 128:256]

    def span(p, ab, n):
        return pl.ds(*FWD[p][ab][n])

    def send_group(p, ab, n):
        arrived = (left_right0, left_right1)[p]
        both = pl.ds(2 * ab, 2)
        send_all(
            lambda d: msg.at[both, span(p, ab, n), d], arrived.at[both, me, span(p, ab, n)],
            fwd_send.at[p, ab, n], fwd_recv.at[p, ab, n],
        )

    def wait_channel(p, ab):
        arrived = (left_right0, left_right1)[p]
        for n in range(len(FWD[p][ab])):
            wait_bytes(arrived.at[pl.ds(2 * ab, 2), :, span(p, ab, n)], fwd_recv.at[p, ab, n])

    def wait_sent(p):
        for ab in range(2):
            for n in range(len(FWD[p][ab])):
                wait_bytes(
                    msg.at[pl.ds(2 * ab, 2), span(p, ab, n), pl.ds(0, CHIPS - 1)], fwd_send.at[p, ab, n])

    def main_cols(src, i, it):
        return src[i, 32 * it:32 * (it + 1), 0:12].reshape(768, 128)

    def mixed_cols(src, i):
        t = src[i, 0:32, 12:18].reshape(384, 128).astype(F32)
        v = src[i, 32:64, 12:18].reshape(384, 128).astype(F32)
        x2[:, 0] = pick(t, v).astype(BF16).reshape(32, 6, 2, 128)
        x2[:, 1] = pltpu.roll(pick(v, t), 64, 1).astype(BF16).reshape(32, 6, 2, 128)
        return x2[...].reshape(768, 128)

    def core_copy(src, dst, i):
        return pltpu.make_async_remote_copy(
            src_ref=src, dst_ref=dst, send_sem=core_send.at[i], recv_sem=core_recv.at[i],
            device_id=sibling, device_id_type=MESH,
        )

    def mix_out(ab):
        src = left_right0
        wait_channel(0, ab)
        for it in range(2):
            xt0[ab, it * 128:(it + 1) * 128] = main_cols(src, ab * 2 + 1, it).T
        xt0[ab, 256:384] = mixed_cols(src, ab * 2 + 1).T
        copy = core_copy(xt0.at[ab], xt0_far.at[ab], ab)
        copy.start()
        for it in range(2):
            xl0[ab, :, it * 128:(it + 1) * 128] = main_cols(src, ab * 2, it)
        xl0[ab, :, 256:384] = mixed_cols(src, ab * 2)

        def contract(right, owner):
            got = jnp.dot(right, xl0[ab], preferred_element_type=F32)
            first = pl.multiple_of(owner * 192, 64)
            for it in range(3):
                piece = got[:, it * 128:(it + 1) * 128].astype(BF16)
                mixed[it, pl.ds(first, 128), :] = piece[0:128]
                mixed[it, pl.ds(first + 384, 128), :] = piece[128:256]
                mixed[it, pl.ds(first + 128, 64), :] = piece[256:320]
                mixed[it, pl.ds(first + 512, 64), :] = piece[320:384]

        contract(xt0[ab], core)
        copy.wait()
        contract(xt0_far[ab], 1 - core)

    def own_rows(ref):
        return jnp.concatenate([ref[0, 0:128], ref[1, 0:128], ref[0, 128:192], ref[1, 128:192]], 0)

    def mix_in(ab):
        src = left_right1
        wait_channel(1, ab)
        for it in range(2):
            xr1[ab, :, it * 128:(it + 1) * 128] = main_cols(src, ab * 2 + 1, it)
        xr1[ab, :, 256:384] = mixed_cols(src, ab * 2 + 1)
        right = core_copy(xr1.at[ab], xr1_far.at[ab], 2 + ab)
        right.start()
        for it in range(2):
            xl1[ab, :, :, :, it * 128:(it + 1) * 128] = main_cols(src, ab * 2, it).reshape(2, 2, 192, 128)
        xl1[ab, :, :, :, 256:384] = mixed_cols(src, ab * 2).reshape(2, 2, 192, 128)
        left = core_copy(xl1.at[ab, :, 1 - core], xl1_far.at[ab], 4 + ab)
        left.start()

        def contract(right, left):
            return lax.dot_general(right, left, (((1,), (1,)), ((), ())), preferred_element_type=F32)

        got = contract(xr1[ab], own_rows(xl1.at[ab, :, core]))
        right.wait()
        left.wait()
        got = got + contract(xr1_far[ab], own_rows(xl1_far.at[ab]))
        for it in range(3):
            mixed[it] = got[:, it * 128:(it + 1) * 128].astype(BF16)

    def send_back(p, ab, n):
        some = pl.ds(*RET[p][ab][n])
        send_all(
            lambda d: ret.at[ab, d, some], (mix0, mix1)[p].at[ab, some, me],
            ret_send.at[p, ab, n], ret_recv.at[p, ab, n],
        )

    def give_back(p, ab):
        for it in range(2):
            ret[ab, it * 32:(it + 1) * 32, 0:12] = mixed[it].reshape(32, 12, 2, 128)
        if ab == 1:
            send_back(p, ab, 0)
            send_back(p, ab, 1)
        x2[...] = mixed[2].reshape(32, 2, 6, 2, 128)
        top = x2[:, 0].reshape(384, 128).astype(F32)
        bot = pltpu.roll(x2[:, 1].reshape(384, 128).astype(F32), 64, 1)
        ret[ab, 0:32, 12:18] = pick(top, bot).astype(BF16).reshape(32, 6, 2, 128)
        ret[ab, 32:64, 12:18] = pick(bot, top).astype(BF16).reshape(32, 6, 2, 128)
        send_back(p, ab, 2 if ab == 1 else 0)

    def wait_back(p, ab, n):
        wait_bytes((mix0, mix1)[p].at[ab, pl.ds(*RET[p][ab][n])], ret_recv.at[p, ab, n])

    def wait_back_sent(p):
        for ab in range(2):
            for n in range(len(RET[p][ab])):
                wait_bytes(ret.at[ab, pl.ds(0, CHIPS - 1), pl.ds(*RET[p][ab][n])], ret_send.at[p, ab, n])

    def mean_rows(values):
        total = jnp.sum(values.reshape(32, 8, 128), 0)
        total = total + pltpu.roll(total, 4, 0)
        total = total + pltpu.roll(total, 2, 0)
        return (total * (1.0 / C)).reshape(1, 8, 128)

    def norm_mix(values, gain):
        centered = values.reshape(32, 8, 128) - mean_rows(values)
        variance = mean_rows(centered * centered)
        return (centered * lax.rsqrt(variance + 1e-05)).reshape(256, 128) * gain

    def finish(p, u):
        mix = (mix0, mix1)[p]
        cols = []
        for e in range(2):
            vals = jnp.concatenate([mix[ab, 2 * u + e].reshape(128, 128) for ab in range(2)], 0).astype(F32)
            cols.append(norm_mix(vals, gain_out[p]).astype(BF16))
        got = jnp.dot(out_a[p], jnp.concatenate(cols, 1), preferred_element_type=F32)
        for e in range(2):
            tp = 2 * u + e
            zt[tp] = (zt[tp].astype(F32) + gate[tp] * got[:, e * 128:(e + 1) * 128]).astype(BF16)

    prepare_in(0)
    for part, (first, last) in enumerate(((0, 6), (6, 9))):
        loads[part].wait()
        rows = slice(*((0, 3072), (3072, 4608))[part])
        work[rows] = pbuf[rows].astype(F32)

        @pl.loop(first, last)
        def _(u):
            for e in range(2):
                load_tiles(2 * u + e, part == 1)
            project(0, u)

    pl.semaphore_wait(barrier, CHIPS)
    send_group(0, 0, 0)
    send_group(0, 1, 0)
    prepare_out(0)
    gates(0)
    prepare_in(1)
    prepare_out(1)
    for ab in range(2):
        mix_out(ab)
        give_back(0, ab)
    wait_sent(0)
    wait_back(0, 0, 0)
    for g in range(3):
        wait_back(0, 1, g)

        @pl.loop(3 * g, 3 * g + 3)
        def _(u):
            finish(0, u)
            project(1, u)

        send_group(1, 0, g)
    send_group(1, 1, 0)
    gates(1)
    wait_back_sent(0)
    for ab in range(2):
        mix_in(ab)
        give_back(1, ab)
    wait_sent(1)
    stores = [
        pltpu.make_async_copy(pbuf.at[pl.ds(a, n)], out.at[pl.ds(a, n)], local.at[2 + i])
        for i, (a, n) in enumerate(((0, 3072), (3072, 1536)))
    ]
    wait_back(1, 0, 0)
    for g in range(3):
        wait_back(1, 1, g)

        @pl.loop(3 * g, 3 * g + 3)
        def _(u):
            finish(1, u)
            for e in range(2):
                store_tiles(2 * u + e, g == 2)

        if g > 0:
            part = g - 1
            rows = slice(*((0, 3072), (3072, 4608))[part])
            pbuf[rows] = work[rows].astype(BF16)
            stores[part].start()
    wait_back_sent(1)
    for store in stores:
        store.wait()


def on_device(pair, norm_in, proj_weight, gate_weight, norm_out, out_weight):
    vmem = pl.BlockSpec(memory_space=pltpu.VMEM)
    hbm = pl.BlockSpec(memory_space=pl.ANY)
    updated = pl.pallas_call(
        kernel,
        out_shape=jax.ShapeDtypeStruct((ROWS * COLS, C), BF16),
        in_specs=[hbm] + [vmem] * 5,
        out_specs=hbm,
        scratch_shapes=[
            pltpu.VMEM((ROWS * COLS, C), BF16),
            pltpu.VMEM((PAIRS, 256, 128), BF16),
            pltpu.VMEM((PAIRS, 256, 128), BF16),
            pltpu.VMEM((PAIRS, 256, 128), F32),
            pltpu.VMEM((4, PAIRS, CHIPS, 2, 128), BF16),
            pltpu.VMEM((4, CHIPS, PAIRS, 2, 128), BF16),
            pltpu.VMEM((4, CHIPS, PAIRS, 2, 128), BF16),
            pltpu.VMEM((2, TOKENS, 384), BF16),
            pltpu.VMEM((2, 384, TOKENS), BF16),
            pltpu.VMEM((2, 384, TOKENS), BF16),
            pltpu.VMEM((2, 2, 2, 192, 384), BF16),
            pltpu.VMEM((2, TOKENS, 384), BF16),
            pltpu.VMEM((2, 2, 192, 384), BF16),
            pltpu.VMEM((2, TOKENS, 384), BF16),
            pltpu.VMEM((3, TOKENS, 128), BF16),
            pltpu.VMEM((2, CHIPS, PAIRS, 2, 128), BF16),
            pltpu.VMEM((2, PAIRS, CHIPS, 2, 128), BF16),
            pltpu.VMEM((2, PAIRS, CHIPS, 2, 128), BF16),
            pltpu.VMEM((ROWS * COLS, 128), F32),
            pltpu.VMEM((1024, 128), F32),
            pltpu.VMEM((1024, 128), F32),
            pltpu.VMEM((2, 1024, 256), BF16),
            pltpu.VMEM((2, 256, 256), BF16),
            pltpu.VMEM((2, 256, 256), BF16),
            pltpu.VMEM((2, 128, 128), F32),
            pltpu.VMEM((2, 256, 128), F32),
            pltpu.VMEM((32, 2, 6, 2, 128), BF16),
            pltpu.SemaphoreType.DMA((2, 2, 3)),
            pltpu.SemaphoreType.DMA((2, 2, 3)),
            pltpu.SemaphoreType.DMA((2, 2, 3)),
            pltpu.SemaphoreType.DMA((2, 2, 3)),
            pltpu.SemaphoreType.DMA((6,)),
            pltpu.SemaphoreType.DMA((6,)),
            pltpu.SemaphoreType.DMA((4,)),
        ],
        compiler_params=pltpu.CompilerParams(
            collective_id=0, has_side_effects=True, vmem_limit_bytes=56 * 2**20
        ),
    )(pair.reshape(ROWS * COLS, C), norm_in, proj_weight, gate_weight, norm_out, out_weight)
    return updated.reshape(ROWS, COLS, C)


def solution(mesh):
    placed = (P("row", "col", None), P(), P(), P(), P(), P())
    return jax.shard_map(
        on_device, mesh=mesh, in_specs=placed, out_specs=P("row", "col", None), check_vma=False
    )
```

time: 117 us -> 110 us (0.940)
  Pallas kernels: 114 us -> 107 us
    pallas_call x1, Pallas kernels: 114 us -> 107 us  [on_device(): pl.pallas_call(kernel, out_shape=jax.ShapeDtypeStruct((ROWS * COLS, C), B...]
where the time goes in v2:
time: 110 us; the launch traced here: 109 us
  Pallas kernels  107 us (97%)
  local copies, waits for them, and re-layouts  2.49 us (2%)
    pallas_call x1, Pallas kernels, on_device(): pl.pallas_call(kernel, out_shape=jax.ShapeDtypeStruct((ROWS * COLS, C), B...  107 us
    unnamed x1, local copies, waits for them, and re-layouts  2.49 us

profile of v2, /device:TPU:1, one launch (start us, length us, event | category | flops | bytes accessed | tf_op | source)
XLA Modules:
  0.0 109.4 jit_solution(8854930664661734353)
XLA Ops:
  0.0 106.9 %shard_map.64 = bf16[4608,128]{1,0:T(8,128)(2,1)} custom-call(bf16[4608,128]{1,0:T(8,128)(2,1)} %bitcast.3, f32[2,128]{1,0:T(2,128)} %norm_in.1, bf16[2,128,512]{2,1,0:T(8,128)(2,1)} %proj_w.1, bf16[2,128,128]{2,1,0:T(8,128)(2,1)} %gate_w.1, f32[2,128]{1,0:T(2,128)} %norm_out.1, bf16[2,128,128]{2,1,0:T(8,128)(2,1)} %out_w.1), custom_call_target="tpu_custom_call" | custom-call | tf_op jit(solution)/shard_map/pallas_call | solution.py:383
  106.9 2.5 %copy.8 = bf16[192,24,128]{2,1,0:T(8,128)(2,1)} copy(bf16[192,24,128]{2,1,0:T(8,128)(2,1)} %bitcast.2) | data formatting | bytes 2359296

commit v3 on v2

--- a/solution.py
+++ b/solution.py
@@ -14,7 +14,7 @@
 CHIPS = 64
 PAIRS = 18
 THIRDS = ((0, 6), (6, 6), (12, 6))
-FWD = ((((0, 18),), ((0, 18),)), (THIRDS, ((0, 18),)))
+FWD = ((THIRDS, ((0, 12), (12, 6))), (THIRDS, ((0, 12), (12, 6))))
 RET = ((((0, 18),), THIRDS), (((0, 18),), THIRDS))
 TOKENS = 768
 
@@ -183,9 +183,13 @@
             fwd_send.at[p, ab, n], fwd_recv.at[p, ab, n],
         )
 
-    def wait_channel(p, ab):
+    def send_all_b(p):
+        for n in range(len(FWD[p][1])):
+            send_group(p, 1, n)
+
+    def wait_channel(p, ab, first=0, last=3):
         arrived = (left_right0, left_right1)[p]
-        for n in range(len(FWD[p][ab])):
+        for n in range(len(FWD[p][ab]))[first:last]:
             wait_bytes(arrived.at[pl.ds(2 * ab, 2), :, span(p, ab, n)], fwd_recv.at[p, ab, n])
 
     def wait_sent(p):
@@ -204,23 +208,28 @@
         x2[:, 1] = pltpu.roll(pick(v, t), 64, 1).astype(BF16).reshape(32, 6, 2, 128)
         return x2[...].reshape(768, 128)
 
+    def columns(src, i, tile):
+        return main_cols(src, i, tile) if tile < 2 else mixed_cols(src, i)
+
     def core_copy(src, dst, i):
         return pltpu.make_async_remote_copy(
             src_ref=src, dst_ref=dst, send_sem=core_send.at[i], recv_sem=core_recv.at[i],
             device_id=sibling, device_id_type=MESH,
         )
 
-    def mix_out(ab):
+    def mix_out(ab, arrive):
         src = left_right0
-        wait_channel(0, ab)
-        for it in range(2):
-            xt0[ab, it * 128:(it + 1) * 128] = main_cols(src, ab * 2 + 1, it).T
-        xt0[ab, 256:384] = mixed_cols(src, ab * 2 + 1).T
-        copy = core_copy(xt0.at[ab], xt0_far.at[ab], ab)
-        copy.start()
-        for it in range(2):
-            xl0[ab, :, it * 128:(it + 1) * 128] = main_cols(src, ab * 2, it)
-        xl0[ab, :, 256:384] = mixed_cols(src, ab * 2)
+        copies = []
+        for part, cols in enumerate((slice(0, 256), slice(256, 384))):
+            arrive(part)
+            for at in range(cols.start, cols.stop, 128):
+                xt0[ab, at:at + 128] = columns(src, ab * 2 + 1, at // 128).T
+            rows = pl.ds(cols.start, cols.stop - cols.start)
+            copy = core_copy(xt0.at[ab, rows], xt0_far.at[ab, rows], 2 * ab + part)
+            copy.start()
+            copies.append(copy)
+            for at in range(cols.start, cols.stop, 128):
+                xl0[ab, :, at:at + 128] = columns(src, ab * 2, at // 128)
 
         def contract(right, owner):
             got = jnp.dot(right, xl0[ab], preferred_element_type=F32)
@@ -233,32 +242,35 @@
                 mixed[it, pl.ds(first + 512, 64), :] = piece[320:384]
 
         contract(xt0[ab], core)
-        copy.wait()
+        for copy in copies:
+            copy.wait()
         contract(xt0_far[ab], 1 - core)
 
     def own_rows(ref):
         return jnp.concatenate([ref[0, 0:128], ref[1, 0:128], ref[0, 128:192], ref[1, 128:192]], 0)
 
-    def mix_in(ab):
+    def mix_in(ab, arrive):
         src = left_right1
-        wait_channel(1, ab)
-        for it in range(2):
-            xr1[ab, :, it * 128:(it + 1) * 128] = main_cols(src, ab * 2 + 1, it)
-        xr1[ab, :, 256:384] = mixed_cols(src, ab * 2 + 1)
-        right = core_copy(xr1.at[ab], xr1_far.at[ab], 2 + ab)
-        right.start()
-        for it in range(2):
-            xl1[ab, :, :, :, it * 128:(it + 1) * 128] = main_cols(src, ab * 2, it).reshape(2, 2, 192, 128)
-        xl1[ab, :, :, :, 256:384] = mixed_cols(src, ab * 2).reshape(2, 2, 192, 128)
-        left = core_copy(xl1.at[ab, :, 1 - core], xl1_far.at[ab], 4 + ab)
-        left.start()
+        copies = []
+        for part, (first, count) in enumerate(((0, 256), (256, 128))):
+            arrive(part)
+            cols = pl.ds(first, count)
+            for at in range(first, first + count, 128):
+                xr1[ab, :, at:at + 128] = columns(src, ab * 2 + 1, at // 128)
+            copies.append(core_copy(xr1.at[ab, :, cols], xr1_far.at[ab, :, cols], 4 + 4 * ab + 2 * part))
+            copies[-1].start()
+            for at in range(first, first + count, 128):
+                xl1[ab, :, :, :, at:at + 128] = columns(src, ab * 2, at // 128).reshape(2, 2, 192, 128)
+            copies.append(core_copy(
+                xl1.at[ab, :, 1 - core, :, cols], xl1_far.at[ab, :, :, cols], 5 + 4 * ab + 2 * part))
+            copies[-1].start()
 
         def contract(right, left):
             return lax.dot_general(right, left, (((1,), (1,)), ((), ())), preferred_element_type=F32)
 
         got = contract(xr1[ab], own_rows(xl1.at[ab, :, core]))
-        right.wait()
-        left.wait()
+        for copy in copies:
+            copy.wait()
         got = got + contract(xr1_far[ab], own_rows(xl1_far.at[ab]))
         for it in range(3):
             mixed[it] = got[:, it * 128:(it + 1) * 128].astype(BF16)
@@ -313,28 +325,39 @@
             tp = 2 * u + e
             zt[tp] = (zt[tp].astype(F32) + gate[tp] * got[:, e * 128:(e + 1) * 128]).astype(BF16)
 
+    def contract_pass(p, mix):
+        def second(part):
+            wait_channel(p, 1, part, part + 1)
+            if part == 0:
+                give_back(p, 0)
+
+        mix(0, lambda part: wait_channel(p, 0, 2 * part, 2 + part))
+        mix(1, second)
+        give_back(p, 1)
+
     prepare_in(0)
-    for part, (first, last) in enumerate(((0, 6), (6, 9))):
-        loads[part].wait()
-        rows = slice(*((0, 3072), (3072, 4608))[part])
-        work[rows] = pbuf[rows].astype(F32)
-
-        @pl.loop(first, last)
+    for g in range(3):
+        if g != 1:
+            part = g // 2
+            loads[part].wait()
+            rows = slice(*((0, 3072), (3072, 4608))[part])
+            work[rows] = pbuf[rows].astype(F32)
+
+        @pl.loop(3 * g, 3 * g + 3)
         def _(u):
             for e in range(2):
-                load_tiles(2 * u + e, part == 1)
+                load_tiles(2 * u + e, g == 2)
             project(0, u)
 
-    pl.semaphore_wait(barrier, CHIPS)
-    send_group(0, 0, 0)
-    send_group(0, 1, 0)
+        if g == 0:
+            pl.semaphore_wait(barrier, CHIPS)
+        send_group(0, 0, g)
+    send_all_b(0)
     prepare_out(0)
     gates(0)
     prepare_in(1)
     prepare_out(1)
-    for ab in range(2):
-        mix_out(ab)
-        give_back(0, ab)
+    contract_pass(0, mix_out)
     wait_sent(0)
     wait_back(0, 0, 0)
     for g in range(3):
@@ -346,12 +369,10 @@
             project(1, u)
 
         send_group(1, 0, g)
-    send_group(1, 1, 0)
+    send_all_b(1)
     gates(1)
     wait_back_sent(0)
-    for ab in range(2):
-        mix_in(ab)
-        give_back(1, ab)
+    contract_pass(1, mix_in)
     wait_sent(1)
     stores = [
         pltpu.make_async_copy(pbuf.at[pl.ds(a, n)], out.at[pl.ds(a, n)], local.at[2 + i])
@@ -417,8 +438,8 @@
             pltpu.SemaphoreType.DMA((2, 2, 3)),
             pltpu.SemaphoreType.DMA((2, 2, 3)),
             pltpu.SemaphoreType.DMA((2, 2, 3)),
-            pltpu.SemaphoreType.DMA((6,)),
-            pltpu.SemaphoreType.DMA((6,)),
+            pltpu.SemaphoreType.DMA((12,)),
+            pltpu.SemaphoreType.DMA((12,)),
             pltpu.SemaphoreType.DMA((4,)),
         ],
         compiler_params=pltpu.CompilerParams(

time: 110 us -> 102 us (0.927)
  Pallas kernels: 107 us -> 99.6 us
    pallas_call x1, Pallas kernels: 107 us -> 99.6 us  [on_device(): pl.pallas_call(kernel, out_shape=jax.ShapeDtypeStruct((ROWS * COLS, C), B...]
where the time goes in v3:
time: 102 us
  Pallas kernels  99.6 us (98%)
  local copies, waits for them, and re-layouts  2.49 us (2%)
    pallas_call x1, Pallas kernels, on_device(): pl.pallas_call(kernel, out_shape=jax.ShapeDtypeStruct((ROWS * COLS, C), B...  99.6 us
    unnamed x1, local copies, waits for them, and re-layouts  2.49 us

profile of v3, /device:TPU:1, one launch (start us, length us, event | category | flops | bytes accessed | tf_op | source)
XLA Modules:
  0.0 102.1 jit_solution(1545662871963325746)
XLA Ops:
  0.0 99.6 %shard_map.64 = bf16[4608,128]{1,0:T(8,128)(2,1)} custom-call(bf16[4608,128]{1,0:T(8,128)(2,1)} %bitcast.3, f32[2,128]{1,0:T(2,128)} %norm_in.1, bf16[2,128,512]{2,1,0:T(8,128)(2,1)} %proj_w.1, bf16[2,128,128]{2,1,0:T(8,128)(2,1)} %gate_w.1, f32[2,128]{1,0:T(2,128)} %norm_out.1, bf16[2,128,128]{2,1,0:T(8,128)(2,1)} %out_w.1), custom_call_target="tpu_custom_call" | custom-call | tf_op jit(solution)/shard_map/pallas_call | solution.py:404
  99.6 2.5 %copy.8 = bf16[192,24,128]{2,1,0:T(8,128)(2,1)} copy(bf16[192,24,128]{2,1,0:T(8,128)(2,1)} %bitcast.2) | data formatting | bytes 2359296

commit v4 on v3

--- a/solution.py
+++ b/solution.py
@@ -374,10 +374,6 @@
     wait_back_sent(0)
     contract_pass(1, mix_in)
     wait_sent(1)
-    stores = [
-        pltpu.make_async_copy(pbuf.at[pl.ds(a, n)], out.at[pl.ds(a, n)], local.at[2 + i])
-        for i, (a, n) in enumerate(((0, 3072), (3072, 1536)))
-    ]
     wait_back(1, 0, 0)
     for g in range(3):
         wait_back(1, 1, g)
@@ -391,11 +387,8 @@
         if g > 0:
             part = g - 1
             rows = slice(*((0, 3072), (3072, 4608))[part])
-            pbuf[rows] = work[rows].astype(BF16)
-            stores[part].start()
+            out[rows] = work[rows].astype(BF16)
     wait_back_sent(1)
-    for store in stores:
-        store.wait()
 
 
 def on_device(pair, norm_in, proj_weight, gate_weight, norm_out, out_weight):
@@ -403,9 +396,9 @@
     hbm = pl.BlockSpec(memory_space=pl.ANY)
     updated = pl.pallas_call(
         kernel,
-        out_shape=jax.ShapeDtypeStruct((ROWS * COLS, C), BF16),
+        out_shape=pltpu.VMEM((ROWS * COLS, C), BF16),
         in_specs=[hbm] + [vmem] * 5,
-        out_specs=hbm,
+        out_specs=vmem,
         scratch_shapes=[
             pltpu.VMEM((ROWS * COLS, C), BF16),
             pltpu.VMEM((PAIRS, 256, 128), BF16),
@@ -440,10 +433,10 @@
             pltpu.SemaphoreType.DMA((2, 2, 3)),
             pltpu.SemaphoreType.DMA((12,)),
             pltpu.SemaphoreType.DMA((12,)),
-            pltpu.SemaphoreType.DMA((4,)),
+            pltpu.SemaphoreType.DMA((2,)),
         ],
         compiler_params=pltpu.CompilerParams(
-            collective_id=0, has_side_effects=True, vmem_limit_bytes=56 * 2**20
+            collective_id=0, has_side_effects=True, vmem_limit_bytes=60 * 2**20
         ),
     )(pair.reshape(ROWS * COLS, C), norm_in, proj_weight, gate_weight, norm_out, out_weight)
     return updated.reshape(ROWS, COLS, C)

time: 102 us -> 99.8 us (0.978)
  local copies, waits for them, and re-layouts: 2.49 us -> 1.02 us
    unnamed x1, local copies, waits for them, and re-layouts: 2.49 us -> 1.02 us
where the time goes in v4:
time: 99.8 us; the launch traced here: 99.6 us
  Pallas kernels  98.6 us (99%)
  local copies, waits for them, and re-layouts  1.02 us (1%)
    pallas_call x1, Pallas kernels, on_device(): pl.pallas_call(kernel, out_shape=pltpu.VMEM((ROWS * COLS, C), BF16), in_s...  98.6 us

profile of v4, /device:TPU:1, one launch (start us, length us, event | category | flops | bytes accessed | tf_op | source)
XLA Modules:
  0.0 99.6 jit_solution(637008581840980040)
XLA Ops:
  0.0 98.6 %shard_map.64 = bf16[4608,128]{1,0:T(8,128)(2,1)S(1)} custom-call(bf16[4608,128]{1,0:T(8,128)(2,1)} %bitcast.3, f32[2,128]{1,0:T(2,128)} %norm_in.1, bf16[2,128,512]{2,1,0:T(8,128)(2,1)} %proj_w.1, bf16[2,128,128]{2,1,0:T(8,128)(2,1)} %gate_w.1, f32[2,128]{1,0:T(2,128)} %norm_out.1, bf16[2,128,128]{2,1,0:T(8,128)(2,1)} %out_w.1), custom_call_target="tpu_custom_call" | custom-call | tf_op jit(solution)/shard_map/pallas_call | solution.py:397
  98.6 1.0 %copy.8 = bf16[192,24,128]{2,1,0:T(8,128)(2,1)} copy(bf16[192,24,128]{2,1,0:T(8,128)(2,1)S(1)} %bitcast.2) | data formatting | bytes 2359296

commit v5 on v4

--- a/solution.py
+++ b/solution.py
@@ -14,8 +14,8 @@
 CHIPS = 64
 PAIRS = 18
 THIRDS = ((0, 6), (6, 6), (12, 6))
-FWD = ((THIRDS, ((0, 12), (12, 6))), (THIRDS, ((0, 12), (12, 6))))
-RET = ((((0, 18),), THIRDS), (((0, 18),), THIRDS))
+FWD = ((THIRDS, ((0, 12), (12, 6))), (((0, 2), (2, 4), (6, 6), (12, 6)), ((0, 12), (12, 6))))
+RET = ((((0, 18),), ((0, 2), (2, 4), (6, 6), (12, 6))), (((0, 18),), THIRDS))
 TOKENS = 768
 
 
@@ -36,7 +36,8 @@
 
 
 def kernel(
-    pair, norm_in, proj_w, gate_w, norm_out, out_w, out,
+    pair, norm_in_hbm, proj_hbm, gate_hbm, norm_out_hbm, out_hbm, out,
+    norm_in, proj_w, gate_w, norm_out, out_w,
     pbuf, zt, nb, gate, msg, left_right0, left_right1, xl0, xt0, xt0_far, xl1, xr1, xl1_far, xr1_far, mixed, ret, mix0, mix1,
     work, wfa, wfb, proj_a, gate_a, out_a, gain_in, gain_out, x2,
     fwd_send, fwd_recv, ret_send, ret_recv, core_send, core_recv, local,
@@ -82,17 +83,22 @@
     def wait_bytes(ref, sem):
         pltpu.make_async_copy(ref, ref, sem).wait()
 
+    barrier = pltpu.get_barrier_semaphore()
+    pl.semaphore_signal(barrier, inc=1, device_id=sibling, device_id_type=MESH)
+    each_peer(lambda py, pc: pl.semaphore_signal(
+        barrier, inc=1, device_id=(py * 2 + core, pc), device_id_type=MESH))
+
     loads = [
         pltpu.make_async_copy(pair.at[pl.ds(a, n)], pbuf.at[pl.ds(a, n)], local.at[i])
         for i, (a, n) in enumerate(((0, 3072), (3072, 1536)))
     ]
-    for load in loads:
+    weights = [
+        pltpu.make_async_copy(src, dst, local.at[2 + i])
+        for i, (src, dst) in enumerate((
+            (norm_in_hbm, norm_in), (proj_hbm, proj_w), (gate_hbm, gate_w), (norm_out_hbm, norm_out), (out_hbm, out_w)))
+    ]
+    for load in weights[:2] + loads + weights[2:]:
         load.start()
-
-    barrier = pltpu.get_barrier_semaphore()
-    pl.semaphore_signal(barrier, inc=1, device_id=sibling, device_id_type=MESH)
-    each_peer(lambda py, pc: pl.semaphore_signal(
-        barrier, inc=1, device_id=(py * 2 + core, pc), device_id_type=MESH))
 
     def picked_gain(ref, p):
         rows = lax.broadcasted_iota(jnp.int32, (2, 128), 0) == p
@@ -187,7 +193,7 @@
         for n in range(len(FWD[p][1])):
             send_group(p, 1, n)
 
-    def wait_channel(p, ab, first=0, last=3):
+    def wait_channel(p, ab, first=0, last=4):
         arrived = (left_right0, left_right1)[p]
         for n in range(len(FWD[p][ab]))[first:last]:
             wait_bytes(arrived.at[pl.ds(2 * ab, 2), :, span(p, ab, n)], fwd_recv.at[p, ab, n])
@@ -231,20 +237,23 @@
             for at in range(cols.start, cols.stop, 128):
                 xl0[ab, :, at:at + 128] = columns(src, ab * 2, at // 128)
 
-        def contract(right, owner):
-            got = jnp.dot(right, xl0[ab], preferred_element_type=F32)
+        def contract(right, owner, tiles):
             first = pl.multiple_of(owner * 192, 64)
+            got = jnp.dot(right[ab, tiles[0] * 128:(tiles[-1] + 1) * 128], xl0[ab], preferred_element_type=F32)
             for it in range(3):
-                piece = got[:, it * 128:(it + 1) * 128].astype(BF16)
-                mixed[it, pl.ds(first, 128), :] = piece[0:128]
-                mixed[it, pl.ds(first + 384, 128), :] = piece[128:256]
-                mixed[it, pl.ds(first + 128, 64), :] = piece[256:320]
-                mixed[it, pl.ds(first + 512, 64), :] = piece[320:384]
-
-        contract(xt0[ab], core)
-        for copy in copies:
-            copy.wait()
-        contract(xt0_far[ab], 1 - core)
+                for n, tile in enumerate(tiles):
+                    piece = got[n * 128:(n + 1) * 128, it * 128:(it + 1) * 128].astype(BF16)
+                    if tile < 2:
+                        mixed[it, pl.ds(first + 384 * tile, 128), :] = piece
+                    else:
+                        mixed[it, pl.ds(first + 128, 64), :] = piece[0:64]
+                        mixed[it, pl.ds(first + 512, 64), :] = piece[64:128]
+
+        contract(xt0, core, (0, 1, 2))
+        copies[0].wait()
+        contract(xt0_far, 1 - core, (0, 1))
+        copies[1].wait()
+        contract(xt0_far, 1 - core, (2,))
 
     def own_rows(ref):
         return jnp.concatenate([ref[0, 0:128], ref[1, 0:128], ref[0, 128:192], ref[1, 128:192]], 0)
@@ -269,9 +278,10 @@
             return lax.dot_general(right, left, (((1,), (1,)), ((), ())), preferred_element_type=F32)
 
         got = contract(xr1[ab], own_rows(xl1.at[ab, :, core]))
-        for copy in copies:
-            copy.wait()
-        got = got + contract(xr1_far[ab], own_rows(xl1_far.at[ab]))
+        for part, cols in enumerate((pl.ds(0, 256), pl.ds(256, 128))):
+            for copy in copies[2 * part:2 * part + 2]:
+                copy.wait()
+            got = got + contract(xr1_far[ab, :, cols], own_rows(xl1_far.at[ab, :, :, cols]))
         for it in range(3):
             mixed[it] = got[:, it * 128:(it + 1) * 128].astype(BF16)
 
@@ -285,15 +295,18 @@
     def give_back(p, ab):
         for it in range(2):
             ret[ab, it * 32:(it + 1) * 32, 0:12] = mixed[it].reshape(32, 12, 2, 128)
-        if ab == 1:
-            send_back(p, ab, 0)
-            send_back(p, ab, 1)
+        parts = list(enumerate(RET[p][ab]))
+        for n, (first, count) in parts:
+            if first + count <= 12:
+                send_back(p, ab, n)
         x2[...] = mixed[2].reshape(32, 2, 6, 2, 128)
         top = x2[:, 0].reshape(384, 128).astype(F32)
         bot = pltpu.roll(x2[:, 1].reshape(384, 128).astype(F32), 64, 1)
         ret[ab, 0:32, 12:18] = pick(top, bot).astype(BF16).reshape(32, 6, 2, 128)
         ret[ab, 32:64, 12:18] = pick(bot, top).astype(BF16).reshape(32, 6, 2, 128)
-        send_back(p, ab, 2 if ab == 1 else 0)
+        for n, (first, count) in parts:
+            if first + count > 12:
+                send_back(p, ab, n)
 
     def wait_back(p, ab, n):
         wait_bytes((mix0, mix1)[p].at[ab, pl.ds(*RET[p][ab][n])], ret_recv.at[p, ab, n])
@@ -331,10 +344,13 @@
             if part == 0:
                 give_back(p, 0)
 
-        mix(0, lambda part: wait_channel(p, 0, 2 * part, 2 + part))
+        cut = len(FWD[p][0]) - 1
+        mix(0, lambda part: wait_channel(p, 0, cut * part, cut + part))
         mix(1, second)
         give_back(p, 1)
 
+    weights[0].wait()
+    weights[1].wait()
     prepare_in(0)
     for g in range(3):
         if g != 1:
@@ -353,6 +369,8 @@
             pl.semaphore_wait(barrier, CHIPS)
         send_group(0, 0, g)
     send_all_b(0)
+    for load in weights[2:]:
+        load.wait()
     prepare_out(0)
     gates(0)
     prepare_in(1)
@@ -360,10 +378,13 @@
     contract_pass(0, mix_out)
     wait_sent(0)
     wait_back(0, 0, 0)
-    for g in range(3):
-        wait_back(0, 1, g)
-
-        @pl.loop(3 * g, 3 * g + 3)
+    waited = 0
+    for g, (start, some) in enumerate(FWD[1][0]):
+        while waited < len(RET[0][1]) and RET[0][1][waited][0] < start + some:
+            wait_back(0, 1, waited)
+            waited += 1
+
+        @pl.loop(start // 2, (start + some) // 2)
         def _(u):
             finish(0, u)
             project(1, u)
@@ -375,18 +396,17 @@
     contract_pass(1, mix_in)
     wait_sent(1)
     wait_back(1, 0, 0)
-    for g in range(3):
+    for g, (start, some) in enumerate(RET[1][1]):
         wait_back(1, 1, g)
 
-        @pl.loop(3 * g, 3 * g + 3)
+        @pl.loop(start // 2, (start + some) // 2)
         def _(u):
             finish(1, u)
             for e in range(2):
-                store_tiles(2 * u + e, g == 2)
-
-        if g > 0:
-            part = g - 1
-            rows = slice(*((0, 3072), (3072, 4608))[part])
+                store_tiles(2 * u + e, start >= 12)
+
+        if start + some in (12, 18):
+            rows = slice(0, 3072) if start < 12 else slice(3072, 4608)
             out[rows] = work[rows].astype(BF16)
     wait_back_sent(1)
 
@@ -397,9 +417,14 @@
     updated = pl.pallas_call(
         kernel,
         out_shape=pltpu.VMEM((ROWS * COLS, C), BF16),
-        in_specs=[hbm] + [vmem] * 5,
+        in_specs=[hbm] * 6,
         out_specs=vmem,
         scratch_shapes=[
+            pltpu.VMEM((2, 128), F32),
+            pltpu.VMEM((2, 128, 512), BF16),
+            pltpu.VMEM((2, 128, 128), BF16),
+            pltpu.VMEM((2, 128), F32),
+            pltpu.VMEM((2, 128, 128), BF16),
             pltpu.VMEM((ROWS * COLS, C), BF16),
             pltpu.VMEM((PAIRS, 256, 128), BF16),
             pltpu.VMEM((PAIRS, 256, 128), BF16),
@@ -427,13 +452,13 @@
             pltpu.VMEM((2, 128, 128), F32),
             pltpu.VMEM((2, 256, 128), F32),
             pltpu.VMEM((32, 2, 6, 2, 128), BF16),
-            pltpu.SemaphoreType.DMA((2, 2, 3)),
-            pltpu.SemaphoreType.DMA((2, 2, 3)),
-            pltpu.SemaphoreType.DMA((2, 2, 3)),
-            pltpu.SemaphoreType.DMA((2, 2, 3)),
+            pltpu.SemaphoreType.DMA((2, 2, 4)),
+            pltpu.SemaphoreType.DMA((2, 2, 4)),
+            pltpu.SemaphoreType.DMA((2, 2, 4)),
+            pltpu.SemaphoreType.DMA((2, 2, 4)),
             pltpu.SemaphoreType.DMA((12,)),
             pltpu.SemaphoreType.DMA((12,)),
-            pltpu.SemaphoreType.DMA((2,)),
+            pltpu.SemaphoreType.DMA((7,)),
         ],
         compiler_params=pltpu.CompilerParams(
             collective_id=0, has_side_effects=True, vmem_limit_bytes=60 * 2**20

time: 99.8 us -> 97.2 us (0.974)
  Pallas kernels: 98.6 us -> 95.9 us
    pallas_call x1, Pallas kernels: 98.6 us -> 95.9 us  [on_device(): pl.pallas_call(kernel, out_shape=pltpu.VMEM((ROWS * COLS, C), BF16), in_s...]
where the time goes in v5:
time: 97.2 us; the launch traced here: 96.9 us
  Pallas kernels  95.9 us (99%)
  local copies, waits for them, and re-layouts  1.02 us (1%)
    pallas_call x1, Pallas kernels, on_device(): pl.pallas_call(kernel, out_shape=pltpu.VMEM((ROWS * COLS, C), BF16), in_s...  95.9 us

profile of v5, /device:TPU:1, one launch (start us, length us, event | category | flops | bytes accessed | tf_op | source)
XLA Modules:
  0.0 96.9 jit_solution(2870968026854726112)
XLA Ops:
  0.0 95.9 %shard_map.64 = bf16[4608,128]{1,0:T(8,128)(2,1)S(1)} custom-call(bf16[4608,128]{1,0:T(8,128)(2,1)} %bitcast.3, f32[2,128]{1,0:T(2,128)} %norm_in_hbm.1, bf16[2,128,512]{2,1,0:T(8,128)(2,1)} %proj_hbm.1, bf16[2,128,128]{2,1,0:T(8,128)(2,1)} %gate_hbm.1, f32[2,128]{1,0:T(2,128)} %norm_out_hbm.1, bf16[2,128,128]{2,1,0:T(8,128)(2,1)} %out_hbm.1), custom_call_target="tpu_custom_call" | custom-call | tf_op jit(solution)/shard_map/pallas_call | solution.py:417
  95.9 1.0 %copy.8 = bf16[192,24,128]{2,1,0:T(8,128)(2,1)} copy(bf16[192,24,128]{2,1,0:T(8,128)(2,1)S(1)} %bitcast.2) | data formatting | bytes 2359296

commit v6 on v5

--- a/solution.py
+++ b/solution.py
@@ -226,6 +226,21 @@
     def mix_out(ab, arrive):
         src = left_right0
         copies = []
+
+        def contract(right, owner, tiles, its):
+            first = pl.multiple_of(owner * 192, 64)
+            rows = slice(tiles[0] * 128, (tiles[-1] + 1) * 128)
+            cols = slice(its[0] * 128, (its[-1] + 1) * 128)
+            got = jnp.dot(right[ab, rows], xl0[ab, :, cols], preferred_element_type=F32)
+            for i, it in enumerate(its):
+                for n, tile in enumerate(tiles):
+                    piece = got[n * 128:(n + 1) * 128, i * 128:(i + 1) * 128].astype(BF16)
+                    if tile < 2:
+                        mixed[it, pl.ds(first + 384 * tile, 128), :] = piece
+                    else:
+                        mixed[it, pl.ds(first + 128, 64), :] = piece[0:64]
+                        mixed[it, pl.ds(first + 512, 64), :] = piece[64:128]
+
         for part, cols in enumerate((slice(0, 256), slice(256, 384))):
             arrive(part)
             for at in range(cols.start, cols.stop, 128):
@@ -236,52 +251,44 @@
             copies.append(copy)
             for at in range(cols.start, cols.stop, 128):
                 xl0[ab, :, at:at + 128] = columns(src, ab * 2, at // 128)
-
-        def contract(right, owner, tiles):
-            first = pl.multiple_of(owner * 192, 64)
-            got = jnp.dot(right[ab, tiles[0] * 128:(tiles[-1] + 1) * 128], xl0[ab], preferred_element_type=F32)
-            for it in range(3):
-                for n, tile in enumerate(tiles):
-                    piece = got[n * 128:(n + 1) * 128, it * 128:(it + 1) * 128].astype(BF16)
-                    if tile < 2:
-                        mixed[it, pl.ds(first + 384 * tile, 128), :] = piece
-                    else:
-                        mixed[it, pl.ds(first + 128, 64), :] = piece[0:64]
-                        mixed[it, pl.ds(first + 512, 64), :] = piece[64:128]
-
-        contract(xt0, core, (0, 1, 2))
-        copies[0].wait()
-        contract(xt0_far, 1 - core, (0, 1))
+            if part == 0:
+                contract(xt0, core, (0, 1), (0, 1))
+                copy.wait()
+                contract(xt0_far, 1 - core, (0, 1), (0, 1))
+
+        contract(xt0, core, (2,), (0, 1, 2))
+        contract(xt0, core, (0, 1), (2,))
+        contract(xt0_far, 1 - core, (0, 1), (2,))
         copies[1].wait()
-        contract(xt0_far, 1 - core, (2,))
+        contract(xt0_far, 1 - core, (2,), (0, 1, 2))
 
     def own_rows(ref):
         return jnp.concatenate([ref[0, 0:128], ref[1, 0:128], ref[0, 128:192], ref[1, 128:192]], 0)
 
     def mix_in(ab, arrive):
         src = left_right1
-        copies = []
+
+        def contract(right, left):
+            return lax.dot_general(right, left, (((1,), (1,)), ((), ())), preferred_element_type=F32)
+
         for part, (first, count) in enumerate(((0, 256), (256, 128))):
             arrive(part)
             cols = pl.ds(first, count)
             for at in range(first, first + count, 128):
                 xr1[ab, :, at:at + 128] = columns(src, ab * 2 + 1, at // 128)
-            copies.append(core_copy(xr1.at[ab, :, cols], xr1_far.at[ab, :, cols], 4 + 4 * ab + 2 * part))
-            copies[-1].start()
+            right = core_copy(xr1.at[ab, :, cols], xr1_far.at[ab, :, cols], 4 + 4 * ab + 2 * part)
+            right.start()
             for at in range(first, first + count, 128):
                 xl1[ab, :, :, :, at:at + 128] = columns(src, ab * 2, at // 128).reshape(2, 2, 192, 128)
-            copies.append(core_copy(
-                xl1.at[ab, :, 1 - core, :, cols], xl1_far.at[ab, :, :, cols], 5 + 4 * ab + 2 * part))
-            copies[-1].start()
-
-        def contract(right, left):
-            return lax.dot_general(right, left, (((1,), (1,)), ((), ())), preferred_element_type=F32)
-
-        got = contract(xr1[ab], own_rows(xl1.at[ab, :, core]))
-        for part, cols in enumerate((pl.ds(0, 256), pl.ds(256, 128))):
-            for copy in copies[2 * part:2 * part + 2]:
-                copy.wait()
+            left = core_copy(
+                xl1.at[ab, :, 1 - core, :, cols], xl1_far.at[ab, :, :, cols], 5 + 4 * ab + 2 * part)
+            left.start()
+            own = contract(xr1[ab, :, cols], own_rows(xl1.at[ab, :, core, :, cols]))
+            got = own if part == 0 else got + own
+            right.wait()
+            left.wait()
             got = got + contract(xr1_far[ab, :, cols], own_rows(xl1_far.at[ab, :, :, cols]))
+
         for it in range(3):
             mixed[it] = got[:, it * 128:(it + 1) * 128].astype(BF16)
 

time: 97.2 us -> 97.9 us (level)
  no operation moved by 1% of the time
where the time goes in v6:
time: 97.9 us; the launch traced here: 97.8 us
  Pallas kernels  96.8 us (99%)
  local copies, waits for them, and re-layouts  1.02 us (1%)
    pallas_call x1, Pallas kernels, on_device(): pl.pallas_call(kernel, out_shape=pltpu.VMEM((ROWS * COLS, C), BF16), in_s...  96.8 us

profile of v6, /device:TPU:1, one launch (start us, length us, event | category | flops | bytes accessed | tf_op | source)
XLA Modules:
  0.0 97.8 jit_solution(6918926367253622047)
XLA Ops:
  0.0 96.8 %shard_map.64 = bf16[4608,128]{1,0:T(8,128)(2,1)S(1)} custom-call(bf16[4608,128]{1,0:T(8,128)(2,1)} %bitcast.3, f32[2,128]{1,0:T(2,128)} %norm_in_hbm.1, bf16[2,128,512]{2,1,0:T(8,128)(2,1)} %proj_hbm.1, bf16[2,128,128]{2,1,0:T(8,128)(2,1)} %gate_hbm.1, f32[2,128]{1,0:T(2,128)} %norm_out_hbm.1, bf16[2,128,128]{2,1,0:T(8,128)(2,1)} %out_hbm.1), custom_call_target="tpu_custom_call" | custom-call | tf_op jit(solution)/shard_map/pallas_call | solution.py:424
  96.8 1.0 %copy.8 = bf16[192,24,128]{2,1,0:T(8,128)(2,1)} copy(bf16[192,24,128]{2,1,0:T(8,128)(2,1)S(1)} %bitcast.2) | data formatting | bytes 2359296

commit v7 on v5

--- a/solution.py
+++ b/solution.py
@@ -260,28 +260,28 @@
 
     def mix_in(ab, arrive):
         src = left_right1
-        copies = []
+
+        def contract(right, left):
+            return lax.dot_general(right, left, (((1,), (1,)), ((), ())), preferred_element_type=F32)
+
         for part, (first, count) in enumerate(((0, 256), (256, 128))):
             arrive(part)
             cols = pl.ds(first, count)
             for at in range(first, first + count, 128):
                 xr1[ab, :, at:at + 128] = columns(src, ab * 2 + 1, at // 128)
-            copies.append(core_copy(xr1.at[ab, :, cols], xr1_far.at[ab, :, cols], 4 + 4 * ab + 2 * part))
-            copies[-1].start()
+            right = core_copy(xr1.at[ab, :, cols], xr1_far.at[ab, :, cols], 4 + 4 * ab + 2 * part)
+            right.start()
             for at in range(first, first + count, 128):
                 xl1[ab, :, :, :, at:at + 128] = columns(src, ab * 2, at // 128).reshape(2, 2, 192, 128)
-            copies.append(core_copy(
-                xl1.at[ab, :, 1 - core, :, cols], xl1_far.at[ab, :, :, cols], 5 + 4 * ab + 2 * part))
-            copies[-1].start()
-
-        def contract(right, left):
-            return lax.dot_general(right, left, (((1,), (1,)), ((), ())), preferred_element_type=F32)
-
-        got = contract(xr1[ab], own_rows(xl1.at[ab, :, core]))
-        for part, cols in enumerate((pl.ds(0, 256), pl.ds(256, 128))):
-            for copy in copies[2 * part:2 * part + 2]:
-                copy.wait()
+            left = core_copy(
+                xl1.at[ab, :, 1 - core, :, cols], xl1_far.at[ab, :, :, cols], 5 + 4 * ab + 2 * part)
+            left.start()
+            own = contract(xr1[ab, :, cols], own_rows(xl1.at[ab, :, core, :, cols]))
+            got = own if part == 0 else got + own
+            right.wait()
+            left.wait()
             got = got + contract(xr1_far[ab, :, cols], own_rows(xl1_far.at[ab, :, :, cols]))
+
         for it in range(3):
             mixed[it] = got[:, it * 128:(it + 1) * 128].astype(BF16)
 

time: 97.2 us -> 98.1 us (level)
  Pallas kernels: 95.9 us -> 97 us
    pallas_call x1, Pallas kernels: 95.9 us -> 97 us  [on_device(): pl.pallas_call(kernel, out_shape=pltpu.VMEM((ROWS * COLS, C), BF16), in_s...]
where the time goes in v7:
time: 98.1 us; the launch traced here: 98 us
  Pallas kernels  97 us (99%)
  local copies, waits for them, and re-layouts  1.02 us (1%)
    pallas_call x1, Pallas kernels, on_device(): pl.pallas_call(kernel, out_shape=pltpu.VMEM((ROWS * COLS, C), BF16), in_s...  97 us

profile of v7, /device:TPU:1, one launch (start us, length us, event | category | flops | bytes accessed | tf_op | source)
XLA Modules:
  0.0 98.0 jit_solution(6175472458379938742)
XLA Ops:
  0.0 97.0 %shard_map.64 = bf16[4608,128]{1,0:T(8,128)(2,1)S(1)} custom-call(bf16[4608,128]{1,0:T(8,128)(2,1)} %bitcast.3, f32[2,128]{1,0:T(2,128)} %norm_in_hbm.1, bf16[2,128,512]{2,1,0:T(8,128)(2,1)} %proj_hbm.1, bf16[2,128,128]{2,1,0:T(8,128)(2,1)} %gate_hbm.1, f32[2,128]{1,0:T(2,128)} %norm_out_hbm.1, bf16[2,128,128]{2,1,0:T(8,128)(2,1)} %out_hbm.1), custom_call_target="tpu_custom_call" | custom-call | tf_op jit(solution)/shard_map/pallas_call | solution.py:417
  97.0 1.0 %copy.8 = bf16[192,24,128]{2,1,0:T(8,128)(2,1)} copy(bf16[192,24,128]{2,1,0:T(8,128)(2,1)S(1)} %bitcast.2) | data formatting | bytes 2359296
